TPU v7x, 32 devices: a whole 2x2x4 slice. The times are simulated.
32 devices in a mesh: grp: 2 (over x), blk: 16 (over z, y, core).
Axes of the slice: x: 2, y: 2, z: 4, core: 2. Of those that a mesh axis runs over, the one named last changes fastest.
Arguments:
- example_grads: bfloat16 [256, 131072], P('grp', 'blk'), parts along dimension 0, may hold values from -6 to 6
- tile_seeds: int32 [256, 8], P('blk'), may hold values from 0 to 16777215
- pair_index: int32 [128, 2], P('grp'), parts along dimension 0, may hold values from 0 to 127
Outputs:
- projected: float32 [4096, 256], P('blk', 'grp'), parts along dimension 1
- scores: float32 [128], P('grp'), parts along dimension 0
There are 2 independent parts, one for each index of `grp`. A program takes and returns all parts, laid end to end along the dimension named above; an argument that names none is the same for every part. Nothing has to cross between parts.
Inputs may be any that keep to these rules, and one draw needn't show every extreme that they name: `pair_index`: column 0 names the query example and column 1 the negative example.
All inputs are finite; a program needn't handle non-finite values.
Results may differ from a plain program's by a relative error of at most 0.0003.
Values sent between devices are 32-bit elements; how exact they have to be, the bound alone decides.
A program may use at most 64 MiB of HBM per device.

v0:
```python
import math

import jax
import jax.numpy as jnp
from jax import lax
from jax.sharding import PartitionSpec as P

TILE = 512


golden_mult = -1640531535
mixer_one = -2048144789
mixer_two = -1028477387


def hashed(seed_value, flat_index):
    mixed = seed_value ^ flat_index * jnp.int32(golden_mult)
    mixed = mixed ^ lax.shift_right_logical(mixed, jnp.int32(16))
    mixed = mixed * jnp.int32(mixer_one)
    mixed = mixed ^ lax.shift_right_logical(mixed, jnp.int32(13))
    mixed = mixed * jnp.int32(mixer_two)
    mixed = mixed ^ lax.shift_right_logical(mixed, jnp.int32(16))
    bit_value = lax.shift_right_logical(mixed, jnp.int32(15)) & jnp.int32(1)
    return jnp.int32(1) - jnp.int32(2) * bit_value


def pair_products(columns, pair_index, examples):
    example_ids = jnp.arange(examples, dtype=jnp.int32)
    pick_query = (pair_index[:, 0][:, None] == example_ids[None, :]).astype(jnp.float32)
    pick_negative = (pair_index[:, 1][:, None] == example_ids[None, :]).astype(jnp.float32)
    query_cols = jnp.dot(columns, pick_query.T, precision=lax.Precision.HIGHEST)
    negative_cols = jnp.dot(columns, pick_negative.T, precision=lax.Precision.HIGHEST)
    return jnp.sum(query_cols * negative_cols, axis=0)


def per_device(example_grads, tile_seeds, pair_index):
    examples, params = example_grads.shape
    devices = lax.axis_size("blk")
    col_total = tile_seeds.shape[1] * TILE
    scaling = 1.0 / math.sqrt(params * devices)
    row_ids = jnp.arange(TILE, dtype=jnp.int32)
    own_count = col_total // devices
    col_ids = jnp.arange(lax.axis_size("blk") * own_count, dtype=jnp.int32)
    flat_index = row_ids[:, None] * TILE + (col_ids % TILE)[None, :]

    def advance(tile_pos, running):
        seed_row = lax.dynamic_index_in_dim(tile_seeds, tile_pos, 0, keepdims=False)
        seed_full = jnp.broadcast_to(seed_row[:, None], (col_total // TILE, TILE)).reshape(
            col_total
        )
        sign_tile = hashed(seed_full[None, :], flat_index).astype(jnp.bfloat16)
        grad_block = lax.dynamic_slice_in_dim(example_grads, tile_pos * TILE, TILE, 1)
        return running + lax.dot_general(
            sign_tile, grad_block, (((0,), (1,)), ((), ())), preferred_element_type=jnp.float32
        )

    running = lax.fori_loop(
        0,
        params // TILE,
        advance,
        jnp.zeros((lax.axis_size("blk") * own_count, examples), jnp.float32),
    )
    own_rows = lax.psum_scatter(running * scaling, "blk", scatter_dimension=0, tiled=True)
    partial_value = pair_products(own_rows, pair_index, examples)
    scores = lax.psum(partial_value, "blk") * (1.0 / math.sqrt(col_total))
    return (own_rows, scores)


def solution(mesh):
    placed = (P("grp", "blk"), P("blk", None), P("grp", None))
    return jax.shard_map(
        per_device,
        mesh=mesh,
        in_specs=placed,
        out_specs=(P("blk", "grp"), P("grp")),
        check_vma=False,
    )
```

profile of v0, /device:TPU:0, one launch (start us, length us, event | category | flops | bytes accessed | tf_op | source)
XLA Modules:
  0.0 209.6 jit_solution(15276359003449174876)
XLA Ops:
  7.2 0.8 copy.5
  8.0 96.4 %while.14 = (s32[]{:T(128)}, f32[4096,128]{1,0:T(8,128)S(1)}, s32[16,8]{1,0:T(8,128)S(1)}, bf16[128,8192]{1,0:T(8,128)(2,1)}, s32[4096]{0:T(1024)S(1)}, /*index=...) while((s32[]{:T(128)}, f32[4096,128]{1,0:T(8,128)S(1)}, s32[16,8]{1,0:T(8,128)S(1)}, ...), condition=%wide.region_1.2_spmd.clone, body=%wide.region_0.1_spmd.clone.sunk | while | flops 571473920 | bytes 4409605 | solution.py:57
  8.1 5.9 %convolution_add_fusion.2 = f32[4096,128]{1,0:T(8,128)S(1)} fusion(s32[4096]{0:T(1024)S(1)} %get-tuple-element.203, s32[512]{0:T(512)S(1)} %get-tuple-element.204, s32[4096]{0:T(1024)S(1)} %bitcast.17, f32[4096,128]{1,0:T(8,128)S(1)} %get-tuple-element.190, pred[]{:T(512)S(6)} %compare.4, bf16[128,8192]{1,0:T(8,128)(2,1)} %get-tuple-element.202, ...), kind=kOutput, calls=%fused_computation.13.clone.1 | convolution fusion | flops 571473920 | bytes 4360197 | tf_op jit(solution)/shard_map/while/body/eval_jaxpr/dot_general | solution.py:53
  14.1 5.9 %convolution_add_fusion.2 = f32[4096,128]{1,0:T(8,128)S(1)} fusion(s32[4096]{0:T(1024)S(1)} %get-tuple-element.203, s32[512]{0:T(512)S(1)} %get-tuple-element.204, s32[4096]{0:T(1024)S(1)} %bitcast.17, f32[4096,128]{1,0:T(8,128)S(1)} %get-tuple-element.190, pred[]{:T(512)S(6)} %compare.4, bf16[128,8192]{1,0:T(8,128)(2,1)} %get-tuple-element.202, ...), kind=kOutput, calls=%fused_computation.13.clone.1 | convolution fusion | flops 571473920 | bytes 4360197 | tf_op jit(solution)/shard_map/while/body/eval_jaxpr/dot_general | solution.py:53
  20.1 5.9 %convolution_add_fusion.2 = f32[4096,128]{1,0:T(8,128)S(1)} fusion(s32[4096]{0:T(1024)S(1)} %get-tuple-element.203, s32[512]{0:T(512)S(1)} %get-tuple-element.204, s32[4096]{0:T(1024)S(1)} %bitcast.17, f32[4096,128]{1,0:T(8,128)S(1)} %get-tuple-element.190, pred[]{:T(512)S(6)} %compare.4, bf16[128,8192]{1,0:T(8,128)(2,1)} %get-tuple-element.202, ...), kind=kOutput, calls=%fused_computation.13.clone.1 | convolution fusion | flops 571473920 | bytes 4360197 | tf_op jit(solution)/shard_map/while/body/eval_jaxpr/dot_general | solution.py:53
  26.2 5.9 %convolution_add_fusion.2 = f32[4096,128]{1,0:T(8,128)S(1)} fusion(s32[4096]{0:T(1024)S(1)} %get-tuple-element.203, s32[512]{0:T(512)S(1)} %get-tuple-element.204, s32[4096]{0:T(1024)S(1)} %bitcast.17, f32[4096,128]{1,0:T(8,128)S(1)} %get-tuple-element.190, pred[]{:T(512)S(6)} %compare.4, bf16[128,8192]{1,0:T(8,128)(2,1)} %get-tuple-element.202, ...), kind=kOutput, calls=%fused_computation.13.clone.1 | convolution fusion | flops 571473920 | bytes 4360197 | tf_op jit(solution)/shard_map/while/body/eval_jaxpr/dot_general | solution.py:53
  32.2 5.9 %convolution_add_fusion.2 = f32[4096,128]{1,0:T(8,128)S(1)} fusion(s32[4096]{0:T(1024)S(1)} %get-tuple-element.203, s32[512]{0:T(512)S(1)} %get-tuple-element.204, s32[4096]{0:T(1024)S(1)} %bitcast.17, f32[4096,128]{1,0:T(8,128)S(1)} %get-tuple-element.190, pred[]{:T(512)S(6)} %compare.4, bf16[128,8192]{1,0:T(8,128)(2,1)} %get-tuple-element.202, ...), kind=kOutput, calls=%fused_computation.13.clone.1 | convolution fusion | flops 571473920 | bytes 4360197 | tf_op jit(solution)/shard_map/while/body/eval_jaxpr/dot_general | solution.py:53
  38.2 5.9 %convolution_add_fusion.2 = f32[4096,128]{1,0:T(8,128)S(1)} fusion(s32[4096]{0:T(1024)S(1)} %get-tuple-element.203, s32[512]{0:T(512)S(1)} %get-tuple-element.204, s32[4096]{0:T(1024)S(1)} %bitcast.17, f32[4096,128]{1,0:T(8,128)S(1)} %get-tuple-element.190, pred[]{:T(512)S(6)} %compare.4, bf16[128,8192]{1,0:T(8,128)(2,1)} %get-tuple-element.202, ...), kind=kOutput, calls=%fused_computation.13.clone.1 | convolution fusion | flops 571473920 | bytes 4360197 | tf_op jit(solution)/shard_map/while/body/eval_jaxpr/dot_general | solution.py:53
  44.2 5.9 %convolution_add_fusion.2 = f32[4096,128]{1,0:T(8,128)S(1)} fusion(s32[4096]{0:T(1024)S(1)} %get-tuple-element.203, s32[512]{0:T(512)S(1)} %get-tuple-element.204, s32[4096]{0:T(1024)S(1)} %bitcast.17, f32[4096,128]{1,0:T(8,128)S(1)} %get-tuple-element.190, pred[]{:T(512)S(6)} %compare.4, bf16[128,8192]{1,0:T(8,128)(2,1)} %get-tuple-element.202, ...), kind=kOutput, calls=%fused_computation.13.clone.1 | convolution fusion | flops 571473920 | bytes 4360197 | tf_op jit(solution)/shard_map/while/body/eval_jaxpr/dot_general | solution.py:53
  50.3 5.9 %convolution_add_fusion.2 = f32[4096,128]{1,0:T(8,128)S(1)} fusion(s32[4096]{0:T(1024)S(1)} %get-tuple-element.203, s32[512]{0:T(512)S(1)} %get-tuple-element.204, s32[4096]{0:T(1024)S(1)} %bitcast.17, f32[4096,128]{1,0:T(8,128)S(1)} %get-tuple-element.190, pred[]{:T(512)S(6)} %compare.4, bf16[128,8192]{1,0:T(8,128)(2,1)} %get-tuple-element.202, ...), kind=kOutput, calls=%fused_computation.13.clone.1 | convolution fusion | flops 571473920 | bytes 4360197 | tf_op jit(solution)/shard_map/while/body/eval_jaxpr/dot_general | solution.py:53
  56.3 5.9 %convolution_add_fusion.2 = f32[4096,128]{1,0:T(8,128)S(1)} fusion(s32[4096]{0:T(1024)S(1)} %get-tuple-element.203, s32[512]{0:T(512)S(1)} %get-tuple-element.204, s32[4096]{0:T(1024)S(1)} %bitcast.17, f32[4096,128]{1,0:T(8,128)S(1)} %get-tuple-element.190, pred[]{:T(512)S(6)} %compare.4, bf16[128,8192]{1,0:T(8,128)(2,1)} %get-tuple-element.202, ...), kind=kOutput, calls=%fused_computation.13.clone.1 | convolution fusion | flops 571473920 | bytes 4360197 | tf_op jit(solution)/shard_map/while/body/eval_jaxpr/dot_general | solution.py:53
  62.3 5.9 %convolution_add_fusion.2 = f32[4096,128]{1,0:T(8,128)S(1)} fusion(s32[4096]{0:T(1024)S(1)} %get-tuple-element.203, s32[512]{0:T(512)S(1)} %get-tuple-element.204, s32[4096]{0:T(1024)S(1)} %bitcast.17, f32[4096,128]{1,0:T(8,128)S(1)} %get-tuple-element.190, pred[]{:T(512)S(6)} %compare.4, bf16[128,8192]{1,0:T(8,128)(2,1)} %get-tuple-element.202, ...), kind=kOutput, calls=%fused_computation.13.clone.1 | convolution fusion | flops 571473920 | bytes 4360197 | tf_op jit(solution)/shard_map/while/body/eval_jaxpr/dot_general | solution.py:53
  68.3 5.9 %convolution_add_fusion.2 = f32[4096,128]{1,0:T(8,128)S(1)} fusion(s32[4096]{0:T(1024)S(1)} %get-tuple-element.203, s32[512]{0:T(512)S(1)} %get-tuple-element.204, s32[4096]{0:T(1024)S(1)} %bitcast.17, f32[4096,128]{1,0:T(8,128)S(1)} %get-tuple-element.190, pred[]{:T(512)S(6)} %compare.4, bf16[128,8192]{1,0:T(8,128)(2,1)} %get-tuple-element.202, ...), kind=kOutput, calls=%fused_computation.13.clone.1 | convolution fusion | flops 571473920 | bytes 4360197 | tf_op jit(solution)/shard_map/while/body/eval_jaxpr/dot_general | solution.py:53
  74.4 5.9 %convolution_add_fusion.2 = f32[4096,128]{1,0:T(8,128)S(1)} fusion(s32[4096]{0:T(1024)S(1)} %get-tuple-element.203, s32[512]{0:T(512)S(1)} %get-tuple-element.204, s32[4096]{0:T(1024)S(1)} %bitcast.17, f32[4096,128]{1,0:T(8,128)S(1)} %get-tuple-element.190, pred[]{:T(512)S(6)} %compare.4, bf16[128,8192]{1,0:T(8,128)(2,1)} %get-tuple-element.202, ...), kind=kOutput, calls=%fused_computation.13.clone.1 | convolution fusion | flops 571473920 | bytes 4360197 | tf_op jit(solution)/shard_map/while/body/eval_jaxpr/dot_general | solution.py:53
  80.4 5.9 %convolution_add_fusion.2 = f32[4096,128]{1,0:T(8,128)S(1)} fusion(s32[4096]{0:T(1024)S(1)} %get-tuple-element.203, s32[512]{0:T(512)S(1)} %get-tuple-element.204, s32[4096]{0:T(1024)S(1)} %bitcast.17, f32[4096,128]{1,0:T(8,128)S(1)} %get-tuple-element.190, pred[]{:T(512)S(6)} %compare.4, bf16[128,8192]{1,0:T(8,128)(2,1)} %get-tuple-element.202, ...), kind=kOutput, calls=%fused_computation.13.clone.1 | convolution fusion | flops 571473920 | bytes 4360197 | tf_op jit(solution)/shard_map/while/body/eval_jaxpr/dot_general | solution.py:53
  86.4 5.9 %convolution_add_fusion.2 = f32[4096,128]{1,0:T(8,128)S(1)} fusion(s32[4096]{0:T(1024)S(1)} %get-tuple-element.203, s32[512]{0:T(512)S(1)} %get-tuple-element.204, s32[4096]{0:T(1024)S(1)} %bitcast.17, f32[4096,128]{1,0:T(8,128)S(1)} %get-tuple-element.190, pred[]{:T(512)S(6)} %compare.4, bf16[128,8192]{1,0:T(8,128)(2,1)} %get-tuple-element.202, ...), kind=kOutput, calls=%fused_computation.13.clone.1 | convolution fusion | flops 571473920 | bytes 4360197 | tf_op jit(solution)/shard_map/while/body/eval_jaxpr/dot_general | solution.py:53
  92.4 5.9 %convolution_add_fusion.2 = f32[4096,128]{1,0:T(8,128)S(1)} fusion(s32[4096]{0:T(1024)S(1)} %get-tuple-element.203, s32[512]{0:T(512)S(1)} %get-tuple-element.204, s32[4096]{0:T(1024)S(1)} %bitcast.17, f32[4096,128]{1,0:T(8,128)S(1)} %get-tuple-element.190, pred[]{:T(512)S(6)} %compare.4, bf16[128,8192]{1,0:T(8,128)(2,1)} %get-tuple-element.202, ...), kind=kOutput, calls=%fused_computation.13.clone.1 | convolution fusion | flops 571473920 | bytes 4360197 | tf_op jit(solution)/shard_map/while/body/eval_jaxpr/dot_general | solution.py:53
  98.5 5.9 %convolution_add_fusion.2 = f32[4096,128]{1,0:T(8,128)S(1)} fusion(s32[4096]{0:T(1024)S(1)} %get-tuple-element.203, s32[512]{0:T(512)S(1)} %get-tuple-element.204, s32[4096]{0:T(1024)S(1)} %bitcast.17, f32[4096,128]{1,0:T(8,128)S(1)} %get-tuple-element.190, pred[]{:T(512)S(6)} %compare.4, bf16[128,8192]{1,0:T(8,128)(2,1)} %get-tuple-element.202, ...), kind=kOutput, calls=%fused_computation.13.clone.1 | convolution fusion | flops 571473920 | bytes 4360197 | tf_op jit(solution)/shard_map/while/body/eval_jaxpr/dot_general | solution.py:53
  104.4 1.5 broadcast_multiply_fusion
  105.9 0.7 copy-done
  106.6 63.8 %reduce-scatter.2.cloned.1.call-done = f32[256,128]{1,0:T(8,128)} async-done(((f32[4096,128]{1,0:T(8,128)}), f32[256,128]{1,0:T(8,128)}) %reduce-scatter.2.cloned.1.call-update) | async-done | bytes 131088 | tf_op jit(solution)/shard_map/reduce_scatter | solution.py:63
  170.4 1.1 fusion.32
  171.5 1.3 fusion.31
  172.8 29.5 %psum.7 = f32[64]{0:T(128)S(1)} all-reduce(f32[64]{0:T(128)S(1)} %fusion.31), channel_id=1, replica_groups=mesh['grp'=2,'blk'=16] {'blk'}, use_global_device_ids=true, to_apply=%region_4.5 | all-reduce | flops 64 | bytes 512 | tf_op jit(solution)/shard_map/psum | solution.py:65
  (56 shorter events, 2.0 us)
Async XLA Ops:
  7.2 163.2 %reduce-scatter.2.cloned.1.call-start = ((), (), s32[]{:S(2)}) async-start(), calls=%async_computation.1 | async-start | bytes 2228224 | tf_op jit(solution)/shard_map/reduce_scatter | solution.py:63
  105.9 0.7 copy-start
Sparse Core Ops, SparseCore 0:
  106.1 64.2 reduce-scatter.1
where the time goes:
time: 210 us
  matrix products  96.8 us (46%)
  waiting for transfers between devices  63.8 us (30%)
  blocking collectives  29.5 us (14%)
  between operations  14.1 us (7%)
  local copies, waits for them, and re-layouts  2.83 us (1%)
    dot_general x16, matrix products, advance(): lax.dot_general(sign_tile, grad_block, (((0,), (1,)), ((), ())), preferre...  94.4 us
    reduce_scatter x1, waiting for transfers between devices, per_device(): lax.psum_scatter(running * scaling, 'blk', scatter_dimension=0, tiled=True)  63.8 us
    psum x1, blocking collectives, per_device(): scores = lax.psum(partial_value, 'blk') * (1.0 / math.sqrt(col_total))  29.5 us
  transfers between devices with their start and end apart: 1, of which 1 were waited for; matrix products, arithmetic and copies ran while one was open for 0% of the time, Pallas kernels for 0%

commit v1 on v0

v1 whole, which is shorter than its diff:
```python
import functools
import math

import jax
import jax.numpy as jnp
from jax import lax
from jax.experimental import pallas as pl
from jax.experimental.pallas import tpu as pltpu
from jax.sharding import PartitionSpec as P

TILE = 512
ROWS = 256

golden_mult = -1640531535
mixer_one = -2048144789
mixer_two = -1028477387


def fill_table(table):
    def rows(start, carry):
        base = pl.multiple_of(start * 8, 8)
        col = lax.broadcasted_iota(jnp.int32, (8, TILE), 0) + base
        row = lax.broadcasted_iota(jnp.int32, (8, TILE), 1)
        mixed = (row * TILE + col) * jnp.int32(golden_mult)
        table[pl.ds(base, 8), :] = mixed ^ lax.shift_right_logical(mixed, jnp.int32(16))
        return carry

    lax.fori_loop(0, TILE // 8, rows, 0)


def signs(entries, seed):
    mixed = (entries ^ seed) * jnp.int32(mixer_one)
    mixed = mixed ^ lax.shift_right_logical(mixed, jnp.int32(13))
    mixed = mixed * jnp.int32(mixer_two)
    mixed = mixed ^ lax.shift_right_logical(mixed, jnp.int32(16))
    low = mixed.astype(jnp.int16)
    return jnp.where(low < 0, jnp.bfloat16(-1), jnp.bfloat16(1))


def kernel(
    devices, scaling,
    seeds, grads, pairs, own_ref, score_ref,
    table, part, sib, summed, arrive, score_send, score_recv,
    sib_s, sib_r, out_s, out_r, sc_s, sc_r,
):
    me = lax.axis_index("blk")
    core = lax.rem(me, 2)
    chip = lax.div(me, 2)
    chips = devices // 2
    sibling = me + 1 - 2 * core
    own, examples = own_ref.shape
    width = 2 * own
    step_rows = min(width, ROWS)
    row_tiles = seeds.shape[0]

    barrier = pltpu.get_barrier_semaphore()

    def greet(shift, carry):
        pl.semaphore_signal(
            barrier, inc=1, device_id={"blk": lax.rem(me + shift, devices)},
            device_id_type=pl.DeviceIdType.MESH,
        )
        return carry

    lax.fori_loop(1, devices, greet, 0)
    fill_table(table)

    def target(step):
        return lax.rem(chip + 1 + step, chips)

    def compute(step):
        start = target(step) * width
        tile_col = lax.div(start, TILE)
        within = lax.rem(start, TILE)

        def row_tile(pos, carry):
            seed = seeds[pos, tile_col]
            seed = seed ^ lax.shift_right_logical(seed, jnp.int32(16))
            block = grads[:, pl.ds(pl.multiple_of(pos * TILE, TILE), TILE)]
            for piece in range(width // step_rows):
                at = pl.multiple_of(within + piece * step_rows, step_rows)
                sign = signs(table[pl.ds(at, step_rows), :], seed)
                add = lax.dot_general(
                    sign, block, (((1,), (1,)), ((), ())),
                    preferred_element_type=jnp.float32,
                )
                rows = pl.ds(piece * step_rows, step_rows)
                part[step, rows, :] += add
            return carry

        part[step] = jnp.zeros((width, examples), jnp.float32)
        lax.fori_loop(0, row_tiles, row_tile, 0)

    def half(which):
        return pl.ds(pl.multiple_of(which * own, own), own)

    def sib_copy(step):
        return pltpu.make_async_remote_copy(
            src_ref=part.at[step, half(1 - core), :],
            dst_ref=sib.at[step],
            send_sem=sib_s.at[step],
            recv_sem=sib_r.at[step],
            device_id={"blk": sibling},
            device_id_type=pl.DeviceIdType.MESH,
        )

    def out_copy(step):
        return pltpu.make_async_remote_copy(
            src_ref=summed.at[step],
            dst_ref=arrive.at[step],
            send_sem=out_s.at[step],
            recv_sem=out_r.at[step],
            device_id={"blk": target(step) * 2 + core},
            device_id_type=pl.DeviceIdType.MESH,
        )

    def forward(step):
        sib_copy(step).wait()
        summed[step] = part[step, half(core), :] + sib[step]
        out_copy(step).start()

    compute(0)
    pl.semaphore_wait(barrier, devices - 1)
    sib_copy(0).start()

    def advance(step, carry):
        compute(step)
        sib_copy(step).start()
        forward(step - 1)
        return carry

    lax.fori_loop(1, chips, advance, 0)
    last = chips - 1
    sib_copy(last).wait()
    own_ref[...] = part[last, half(core), :] + sib[last]

    def gather(step, carry):
        out_copy(step).wait()
        own_ref[...] += arrive[step]
        return carry

    lax.fori_loop(0, last, gather, 0)

    ids = lax.broadcasted_iota(jnp.int32, (pairs.shape[0], examples), 1)
    columns = own_ref[...] * scaling

    def pick(which):
        chosen = jnp.where(pairs[:, which : which + 1] == ids, 1.0, 0.0)
        return lax.dot_general(
            columns, chosen, (((1,), (1,)), ((), ())),
            precision=lax.Precision.HIGHEST,
            preferred_element_type=jnp.float32,
        )

    share = jnp.sum(pick(0) * pick(1), axis=0, keepdims=True)
    score_send[...] = jnp.zeros_like(score_send)
    score_send[0:1, 0 : pairs.shape[0]] = share

    def score_copy(shift):
        return pltpu.make_async_remote_copy(
            src_ref=score_send,
            dst_ref=score_recv.at[shift],
            send_sem=sc_s.at[shift],
            recv_sem=sc_r.at[shift],
            device_id={"blk": lax.rem(me + shift, devices)},
            device_id_type=pl.DeviceIdType.MESH,
        )

    def score_start(shift, carry):
        score_copy(shift).start()
        return carry

    lax.fori_loop(1, devices, score_start, 0)
    score_ref[...] = score_send[...]

    def score_finish(shift, carry):
        score_copy(shift).wait()
        score_ref[...] += score_recv[shift]
        return carry

    lax.fori_loop(1, devices, score_finish, 0)


def per_device(example_grads, tile_seeds, pair_index):
    examples, params = example_grads.shape
    devices = lax.axis_size("blk")
    col_total = tile_seeds.shape[1] * TILE
    scaling = 1.0 / math.sqrt(params * devices)
    own = col_total // devices
    chips = devices // 2
    pairs = pair_index.shape[0]
    lanes = -(-pairs // 128) * 128
    vmem = pl.BlockSpec(memory_space=pltpu.VMEM)
    own_rows, shares = pl.pallas_call(
        functools.partial(kernel, devices, scaling),
        out_shape=(
            jax.ShapeDtypeStruct((own, examples), jnp.float32),
            jax.ShapeDtypeStruct((8, lanes), jnp.float32),
        ),
        in_specs=[pl.BlockSpec(memory_space=pltpu.SMEM), vmem, vmem],
        out_specs=(vmem, vmem),
        scratch_shapes=[
            pltpu.VMEM((TILE, TILE), jnp.int32),
            pltpu.VMEM((chips, 2 * own, examples), jnp.float32),
            pltpu.VMEM((chips, own, examples), jnp.float32),
            pltpu.VMEM((chips, own, examples), jnp.float32),
            pltpu.VMEM((chips, own, examples), jnp.float32),
            pltpu.VMEM((8, lanes), jnp.float32),
            pltpu.VMEM((devices, 8, lanes), jnp.float32),
            pltpu.SemaphoreType.DMA((chips,)),
            pltpu.SemaphoreType.DMA((chips,)),
            pltpu.SemaphoreType.DMA((chips,)),
            pltpu.SemaphoreType.DMA((chips,)),
            pltpu.SemaphoreType.DMA((devices,)),
            pltpu.SemaphoreType.DMA((devices,)),
        ],
        compiler_params=pltpu.CompilerParams(
            collective_id=0, has_side_effects=True, vmem_limit_bytes=40 * 1024 * 1024
        ),
        cost_estimate=pl.CostEstimate(
            flops=2 * col_total * params * examples,
            bytes_accessed=2 * params * examples,
            transcendentals=0,
        ),
    )(tile_seeds, example_grads, pair_index)
    scores = shares[0, :pairs] * (1.0 / math.sqrt(col_total))
    return (own_rows * scaling, scores)


def solution(mesh):
    placed = (P("grp", "blk"), P("blk", None), P("grp", None))
    return jax.shard_map(
        per_device,
        mesh=mesh,
        in_specs=placed,
        out_specs=(P("blk", "grp"), P("grp")),
        check_vma=False,
    )
```

time: 210 us -> 75.2 us (0.36)
  matrix products: 96.8 us -> 0 us
  Pallas kernels: 0 us -> 70.1 us
  waiting for transfers between devices: 63.8 us -> 0 us
  blocking collectives: 29.5 us -> 0 us
  between operations: 14.1 us -> 0.64 us
    dot_general x18 -> x0, matrix products: 96.8 us -> none  [the longest x16 94.4 us: advance(): lax.dot_general(sign_tile, grad_block, (((0,), (1,)), ((), ())), preferre...]
    pallas_call x0 -> x1, Pallas kernels: none -> 70.1 us  [per_device(): pl.pallas_call(functools.partial(kernel, devices, scaling), out_shape=(ja...]
    reduce_scatter x1 -> x0, waiting for transfers between devices: 63.8 us -> none  [per_device(): lax.psum_scatter(running * scaling, 'blk', scatter_dimension=0, tiled=True)]
    psum x1 -> x0, blocking collectives: 29.5 us -> none  [per_device(): scores = lax.psum(partial_value, 'blk') * (1.0 / math.sqrt(col_total))]
  transfers between devices with their start and end apart: 1 -> 0, of which waited for: 1 -> 0; matrix products, arithmetic and copies ran while one was open for 0% -> 0% of each run, Pallas kernels for 0% -> 0%
where the time goes in v1:
time: 75.2 us; the launch traced here: 75 us
  Pallas kernels  70.1 us (93%)
  local copies, waits for them, and re-layouts  3.12 us (4%)
  other arithmetic  1.18 us (2%)
    pallas_call x1, Pallas kernels, per_device(): pl.pallas_call(functools.partial(kernel, devices, scaling), out_shape=(ja...  70.1 us
    unnamed x4, local copies, waits for them, and re-layouts  3.12 us

profile of v1, /device:TPU:0, one launch (start us, length us, event | category | flops | bytes accessed | tf_op | source)
XLA Modules:
  0.0 75.0 jit_solution(5565761669248108229)
XLA Ops:
  0.6 0.8 %copy.5.seeds = s32[16,8]{1,0:T(8,128)S(1)} copy(s32[16,8]{0,1:T(8,128)} %param.4) | data formatting | bytes 1024 | tf_op args[1]
  1.4 0.8 %copy.6.pairs = s32[64,2]{1,0:T(8,128)S(1)} copy(s32[64,2]{0,1:T(2,128)} %param.5) | data formatting | bytes 1024 | tf_op args[2]
  2.2 0.0 copy-start
  2.2 1.6 %copy-done = bf16[128,8192]{1,0:T(8,128)(2,1)S(1)} copy-done((bf16[128,8192]{1,0:T(8,128)(2,1)S(1)}, bf16[128,8192]{1,0:T(8,128)(2,1)}, u32[]{:S(2)}) %copy-start) | copy-done | bytes 2097176
  3.7 70.1 %shard_map.50 = (f32[256,128]{1,0:T(8,128)S(1)}, f32[8,128]{1,0:T(8,128)S(1)}) custom-call(s32[16,8]{1,0:T(8,128)S(1)} %copy.5.seeds, bf16[128,8192]{1,0:T(8,128)(2,1)S(1)} %copy-done, s32[64,2]{1,0:T(8,128)S(1)} %copy.6.pairs), custom_call_target="tpu_custom_call" | custom-call | flops 8589934592 | bytes 2097152 | tf_op jit(solution)/shard_map/pallas_call | solution.py:194
  73.8 0.7 broadcast_multiply_fusion
  74.5 0.5 multiply_bitcast_fusion
Async XLA Ops:
  2.2 1.6 %copy-start = (bf16[128,8192]{1,0:T(8,128)(2,1)S(1)}, bf16[128,8192]{1,0:T(8,128)(2,1)}, u32[]{:S(2)}) copy-start(bf16[128,8192]{1,0:T(8,128)(2,1)} %grads.1) | copy-start | bytes 6291460

commit v2 on v1

--- a/solution.py
+++ b/solution.py
@@ -9,7 +9,7 @@
 from jax.sharding import PartitionSpec as P
 
 TILE = 512
-ROWS = 256
+ROWS = 16
 
 golden_mult = -1640531535
 mixer_one = -2048144789
@@ -39,8 +39,8 @@
 
 def kernel(
     devices, scaling,
-    seeds, grads, pairs, own_ref, score_ref,
-    table, part, sib, summed, arrive, score_send, score_recv,
+    seeds_in, grads_in, pairs_in, own_ref, score_ref,
+    seeds, grads, pairs, in_sem, table, even, odd, part, sib, summed, arrive, score_send, score_recv,
     sib_s, sib_r, out_s, out_r, sc_s, sc_r,
 ):
     me = lax.axis_index("blk")
@@ -50,8 +50,16 @@
     sibling = me + 1 - 2 * core
     own, examples = own_ref.shape
     width = 2 * own
-    step_rows = min(width, ROWS)
-    row_tiles = seeds.shape[0]
+    row_tiles = seeds.shape[1]
+
+    loads = [
+        pltpu.make_async_copy(source, held, in_sem.at[place])
+        for place, (source, held) in enumerate(
+            ((seeds_in, seeds), (grads_in, grads), (pairs_in, pairs))
+        )
+    ]
+    for load in loads:
+        load.start()
 
     barrier = pltpu.get_barrier_semaphore()
 
@@ -68,28 +76,38 @@
     def target(step):
         return lax.rem(chip + 1 + step, chips)
 
+    def hash_tile(step, pos, signs_ref):
+        start = target(step + lax.div(pos, row_tiles)) * width
+        seed = seeds[lax.div(start, TILE), lax.rem(pos, row_tiles)]
+        seed = seed ^ lax.shift_right_logical(seed, jnp.int32(16))
+        within = 0 if width == TILE else lax.rem(start, TILE)
+        for piece in range(width // ROWS):
+            at = within + piece * ROWS
+            if width != TILE:
+                at = pl.multiple_of(at, ROWS)
+            signs_ref[piece * ROWS : (piece + 1) * ROWS, :] = signs(
+                table[pl.ds(at, ROWS), :], seed
+            )
+
+    def multiply(step, pos, signs_ref):
+        block = grads[:, pl.ds(pl.multiple_of(pos * TILE, TILE), TILE)]
+        part[step] += lax.dot_general(
+            signs_ref[...], block, (((1,), (1,)), ((), ())),
+            preferred_element_type=jnp.float32,
+        )
+
     def compute(step):
-        start = target(step) * width
-        tile_col = lax.div(start, TILE)
-        within = lax.rem(start, TILE)
-
-        def row_tile(pos, carry):
-            seed = seeds[pos, tile_col]
-            seed = seed ^ lax.shift_right_logical(seed, jnp.int32(16))
-            block = grads[:, pl.ds(pl.multiple_of(pos * TILE, TILE), TILE)]
-            for piece in range(width // step_rows):
-                at = pl.multiple_of(within + piece * step_rows, step_rows)
-                sign = signs(table[pl.ds(at, step_rows), :], seed)
-                add = lax.dot_general(
-                    sign, block, (((1,), (1,)), ((), ())),
-                    preferred_element_type=jnp.float32,
-                )
-                rows = pl.ds(piece * step_rows, step_rows)
-                part[step, rows, :] += add
+        part[step] = jnp.zeros((width, examples), jnp.float32)
+
+        def two_tiles(index, carry):
+            pos = index * 2
+            hash_tile(step, pos + 1, odd)
+            multiply(step, pos, even)
+            hash_tile(step, pos + 2, even)
+            multiply(step, pos + 1, odd)
             return carry
 
-        part[step] = jnp.zeros((width, examples), jnp.float32)
-        lax.fori_loop(0, row_tiles, row_tile, 0)
+        lax.fori_loop(0, row_tiles // 2, two_tiles, 0)
 
     def half(which):
         return pl.ds(pl.multiple_of(which * own, own), own)
@@ -119,6 +137,10 @@
         summed[step] = part[step, half(core), :] + sib[step]
         out_copy(step).start()
 
+    loads[0].wait()
+    hash_tile(0, 0, even)
+    loads[1].wait()
+    loads[2].wait()
     compute(0)
     pl.semaphore_wait(barrier, devices - 1)
     sib_copy(0).start()
@@ -141,20 +163,21 @@
 
     lax.fori_loop(0, last, gather, 0)
 
-    ids = lax.broadcasted_iota(jnp.int32, (pairs.shape[0], examples), 1)
+    count = pairs.shape[1]
+    ids = lax.broadcasted_iota(jnp.int32, (examples, count), 0)
     columns = own_ref[...] * scaling
 
     def pick(which):
-        chosen = jnp.where(pairs[:, which : which + 1] == ids, 1.0, 0.0)
+        chosen = jnp.where(pairs[which : which + 1, :] == ids, 1.0, 0.0)
         return lax.dot_general(
-            columns, chosen, (((1,), (1,)), ((), ())),
+            columns, chosen, (((1,), (0,)), ((), ())),
             precision=lax.Precision.HIGHEST,
             preferred_element_type=jnp.float32,
         )
 
     share = jnp.sum(pick(0) * pick(1), axis=0, keepdims=True)
     score_send[...] = jnp.zeros_like(score_send)
-    score_send[0:1, 0 : pairs.shape[0]] = share
+    score_send[0:1, 0:count] = share
 
     def score_copy(shift):
         return pltpu.make_async_remote_copy(
@@ -197,10 +220,16 @@
             jax.ShapeDtypeStruct((own, examples), jnp.float32),
             jax.ShapeDtypeStruct((8, lanes), jnp.float32),
         ),
-        in_specs=[pl.BlockSpec(memory_space=pltpu.SMEM), vmem, vmem],
+        in_specs=[pl.BlockSpec(memory_space=pl.ANY)] * 3,
         out_specs=(vmem, vmem),
         scratch_shapes=[
+            pltpu.SMEM(tile_seeds.shape[::-1], jnp.int32),
+            pltpu.VMEM((examples, params), example_grads.dtype),
+            pltpu.VMEM(pair_index.shape[::-1], jnp.int32),
+            pltpu.SemaphoreType.DMA((3,)),
             pltpu.VMEM((TILE, TILE), jnp.int32),
+            pltpu.VMEM((2 * own, TILE), jnp.bfloat16),
+            pltpu.VMEM((2 * own, TILE), jnp.bfloat16),
             pltpu.VMEM((chips, 2 * own, examples), jnp.float32),
             pltpu.VMEM((chips, own, examples), jnp.float32),
             pltpu.VMEM((chips, own, examples), jnp.float32),
@@ -215,14 +244,14 @@
             pltpu.SemaphoreType.DMA((devices,)),
         ],
         compiler_params=pltpu.CompilerParams(
-            collective_id=0, has_side_effects=True, vmem_limit_bytes=40 * 1024 * 1024
+            collective_id=0, has_side_effects=True, vmem_limit_bytes=60 * 1024 * 1024
         ),
         cost_estimate=pl.CostEstimate(
             flops=2 * col_total * params * examples,
             bytes_accessed=2 * params * examples,
             transcendentals=0,
         ),
-    )(tile_seeds, example_grads, pair_index)
+    )(tile_seeds.T, example_grads, pair_index.T)
     scores = shares[0, :pairs] * (1.0 / math.sqrt(col_total))
     return (own_rows * scaling, scores)
 

time: 75.2 us -> 67.4 us (0.90)
  Pallas kernels: 70.1 us -> 63.8 us
  local copies, waits for them, and re-layouts: 3.12 us -> 0 us
  other arithmetic: 1.18 us -> 2.77 us
    pallas_call x1, Pallas kernels: 70.1 us -> 63.8 us  [per_device(): pl.pallas_call(functools.partial(kernel, devices, scaling), out_shape=(ja...]
    unnamed x4 -> x0, local copies, waits for them, and re-layouts: 3.12 us -> none
    mul x1, other arithmetic: 0.67 us -> 1.57 us  [per_device(): return (own_rows * scaling, scores)]
where the time goes in v2:
time: 67.4 us; the launch traced here: 67.2 us
  Pallas kernels  63.8 us (95%)
  other arithmetic  2.77 us (4%)
    pallas_call x1, Pallas kernels, per_device(): pl.pallas_call(functools.partial(kernel, devices, scaling), out_shape=(ja...  63.8 us
    mul x1, other arithmetic, per_device(): return (own_rows * scaling, scores)  1.57 us

profile of v2, /device:TPU:0, one launch (start us, length us, event | category | flops | bytes accessed | tf_op | source)
XLA Modules:
  0.0 67.2 jit_solution(9881398114639384185)
XLA Ops:
  0.6 63.8 %shard_map.50 = (f32[256,128]{1,0:T(8,128)}, f32[8,128]{1,0:T(8,128)}) custom-call(s32[8,16]{1,0:T(8,128)} %bitcast.4, bf16[128,8192]{1,0:T(8,128)(2,1)} %grads_in.1, s32[2,64]{1,0:T(2,128)} %bitcast.5), custom_call_target="tpu_custom_call" | custom-call | flops 8589934592 | bytes 2097152 | tf_op jit(solution)/shard_map/pallas_call | solution.py:217
  64.4 1.6 %broadcast_multiply_fusion = f32[256,128]{1,0:T(8,128)} fusion(f32[256,128]{1,0:T(8,128)} %get-tuple-element.4), kind=kLoop, calls=%fused_computation | loop fusion | flops 32768 | bytes 262144 | tf_op jit(solution)/shard_map/mul | solution.py:256
  66.0 1.2 %multiply_bitcast_fusion = f32[64]{0:T(128)} fusion(f32[8,128]{1,0:T(8,128)} %get-tuple-element.5), kind=kLoop, calls=%fused_computation.1 | loop fusion | flops 64 | bytes 512 | tf_op jit(solution)/shard_map/mul | solution.py:255

commit v3 on v2

--- a/solution.py
+++ b/solution.py
@@ -76,12 +76,13 @@
     def target(step):
         return lax.rem(chip + 1 + step, chips)
 
-    def hash_tile(step, pos, signs_ref):
+    def hash_tile(step, pos, signs_ref, first=0, parts=1):
         start = target(step + lax.div(pos, row_tiles)) * width
         seed = seeds[lax.div(start, TILE), lax.rem(pos, row_tiles)]
         seed = seed ^ lax.shift_right_logical(seed, jnp.int32(16))
         within = 0 if width == TILE else lax.rem(start, TILE)
-        for piece in range(width // ROWS):
+        pieces = width // ROWS
+        for piece in range(pieces * first // parts, pieces * (first + 1) // parts):
             at = within + piece * ROWS
             if width != TILE:
                 at = pl.multiple_of(at, ROWS)
@@ -89,25 +90,30 @@
                 table[pl.ds(at, ROWS), :], seed
             )
 
-    def multiply(step, pos, signs_ref):
-        block = grads[:, pl.ds(pl.multiple_of(pos * TILE, TILE), TILE)]
-        part[step] += lax.dot_general(
-            signs_ref[...], block, (((1,), (1,)), ((), ())),
-            preferred_element_type=jnp.float32,
-        )
-
-    def compute(step):
+    def multiply_and_hash(step, pos, ready, filled):
+        depth = TILE // 2
+        for part_pos in range(2):
+            at = pl.multiple_of(pos * TILE + part_pos * depth, depth)
+            part[step] += lax.dot_general(
+                ready[:, part_pos * depth : (part_pos + 1) * depth],
+                grads[:, pl.ds(at, depth)],
+                (((1,), (1,)), ((), ())),
+                preferred_element_type=jnp.float32,
+            )
+            hash_tile(step, pos + 1, filled, part_pos, 2)
+
+    def compute(step, between):
         part[step] = jnp.zeros((width, examples), jnp.float32)
 
         def two_tiles(index, carry):
-            pos = index * 2
-            hash_tile(step, pos + 1, odd)
-            multiply(step, pos, even)
-            hash_tile(step, pos + 2, even)
-            multiply(step, pos + 1, odd)
+            multiply_and_hash(step, index * 2, even, odd)
+            multiply_and_hash(step, index * 2 + 1, odd, even)
             return carry
 
-        lax.fori_loop(0, row_tiles // 2, two_tiles, 0)
+        rounds = row_tiles // 2
+        lax.fori_loop(0, rounds // 4, two_tiles, 0)
+        between()
+        lax.fori_loop(rounds // 4, rounds, two_tiles, 0)
 
     def half(which):
         return pl.ds(pl.multiple_of(which * own, own), own)
@@ -141,14 +147,13 @@
     hash_tile(0, 0, even)
     loads[1].wait()
     loads[2].wait()
-    compute(0)
+    compute(0, lambda: None)
     pl.semaphore_wait(barrier, devices - 1)
     sib_copy(0).start()
 
     def advance(step, carry):
-        compute(step)
+        compute(step, lambda: forward(step - 1))
         sib_copy(step).start()
-        forward(step - 1)
         return carry
 
     lax.fori_loop(1, chips, advance, 0)

time: 67.4 us -> 64.4 us (0.955)
  Pallas kernels: 63.8 us -> 60.8 us
    pallas_call x1, Pallas kernels: 63.8 us -> 60.8 us  [per_device(): pl.pallas_call(functools.partial(kernel, devices, scaling), out_shape=(ja...]
where the time goes in v3:
time: 64.4 us; the launch traced here: 64.2 us
  Pallas kernels  60.8 us (94%)
  other arithmetic  2.77 us (4%)
    pallas_call x1, Pallas kernels, per_device(): pl.pallas_call(functools.partial(kernel, devices, scaling), out_shape=(ja...  60.8 us
    mul x1, other arithmetic, per_device(): return (own_rows * scaling, scores)  1.57 us

profile of v3, /device:TPU:0, one launch (start us, length us, event | category | flops | bytes accessed | tf_op | source)
XLA Modules:
  0.0 64.2 jit_solution(17496814717729702459)
XLA Ops:
  0.6 60.8 %shard_map.50 = (f32[256,128]{1,0:T(8,128)}, f32[8,128]{1,0:T(8,128)}) custom-call(s32[8,16]{1,0:T(8,128)} %bitcast.4, bf16[128,8192]{1,0:T(8,128)(2,1)} %grads_in.1, s32[2,64]{1,0:T(2,128)} %bitcast.5), custom_call_target="tpu_custom_call" | custom-call | flops 8589934592 | bytes 2097152 | tf_op jit(solution)/shard_map/pallas_call | solution.py:222
  61.4 1.6 %broadcast_multiply_fusion = f32[256,128]{1,0:T(8,128)} fusion(f32[256,128]{1,0:T(8,128)} %get-tuple-element.4), kind=kLoop, calls=%fused_computation | loop fusion | flops 32768 | bytes 262144 | tf_op jit(solution)/shard_map/mul | solution.py:261
  63.0 1.2 %multiply_bitcast_fusion = f32[64]{0:T(128)} fusion(f32[8,128]{1,0:T(8,128)} %get-tuple-element.5), kind=kLoop, calls=%fused_computation.1 | loop fusion | flops 64 | bytes 512 | tf_op jit(solution)/shard_map/mul | solution.py:260
